TPU v7x, 256 devices: a whole 4x4x8 slice. The times are simulated.
256 devices in a mesh: dp: 8 (over y, z_hi), owner: 32 (over x, z_lo, core).
Axes of the slice: x: 4, y: 4, z: 8 (z_hi: 2, z_lo: 4; z = z_hi * 4 + z_lo), core: 2. Of those that a mesh axis runs over, the one named last changes fastest.
Arguments:
- grad_parts: bfloat16 [8, 128, 512, 512], P('dp', None, 'owner'), may hold values from -2.5 to 2.5
- stats: float32 [256, 512, 512], P(('dp', 'owner')), may hold values from -10 to 12, as said below
- roots: bfloat16 [256, 512, 512], P(('dp', 'owner')), may hold values from -0.25 to 0.25
- refresh: int32 [128], P('dp'), may hold values 0 or 1
Outputs:
- new_stats: float32 [256, 512, 512], P(('dp', 'owner'))
- new_roots: bfloat16 [256, 512, 512], P(('dp', 'owner'))
- update: bfloat16 [128, 512, 512], P('dp', 'owner')
Inputs may be any that keep to these rules, and one draw needn't show every extreme that they name: Every stats matrix is symmetric positive definite.
All inputs are finite; a program needn't handle non-finite values. No bound on the sum of `refresh` on one device may be relied on, other than what follows from the above.
Results may differ from a plain program's by a relative error of at most 0.015.
Values may be sent and summed in bfloat16 or wider, within the bound.
A program may use at most 64 MiB of HBM per device.

v0:
```python
import jax
import jax.numpy as jnp
from jax import lax
from jax.sharding import PartitionSpec as P

ITERS = 5


BETA = 0.8


def split_up(x, dim, peers):
    before, after = (x.shape[:dim], x.shape[dim + 1 :])
    return jnp.moveaxis(x.reshape(*before, peers, -1, *after), dim, 0)


def summed_on_arrival(x, axis, dim):
    pieces = split_up(x, dim, lax.axis_size(axis))
    arrived = lax.all_to_all(pieces, axis, split_axis=0, concat_axis=0, tiled=True)
    return arrived.astype(jnp.float32).sum(axis=0)


def partner_2(value, axis, stride):
    mask = 2**stride
    pairs = [(source, source ^ mask) for source in range(lax.axis_size(axis))]
    return lax.ppermute(value, axis, pairs)


def inverse_root(matrix):
    size = matrix.shape[0]
    eye = jnp.eye(size, dtype=jnp.float32)
    scale = jnp.sqrt(jnp.sum(matrix * matrix) + 1e-06)
    current = matrix / scale
    result = eye * scale ** (-0.25)
    for step in range(ITERS):
        factor = (5.0 * eye - current) / 4.0
        result = jnp.dot(result, factor, precision=lax.Precision.HIGHEST)
        if step + 1 < ITERS:
            square = jnp.dot(factor, factor, precision=lax.Precision.HIGHEST)
            fourth = jnp.dot(square, square, precision=lax.Precision.HIGHEST)
            current = jnp.dot(fourth, current, precision=lax.Precision.HIGHEST)
    return result


def local(grad_parts, stats, roots, refresh):
    summed = summed_on_arrival(grad_parts, "dp", 1)
    grad = summed[0].astype(jnp.bfloat16)
    blocks, rows, width = grad.shape
    owner = lax.axis_index("owner")
    side = owner % 2
    flag = lax.dynamic_index_in_dim(refresh, owner // 2, 0, keepdims=False)
    doubled = jnp.repeat(grad, 2, axis=0)
    whole = lax.all_to_all(doubled, "owner", split_axis=0, concat_axis=1, tiled=True)[0]
    oriented = jnp.where(side == 0, whole, whole.T)
    gram = jnp.dot(oriented, oriented.T, preferred_element_type=jnp.float32)
    partner = partner_2(roots, "owner", 0)[0]
    left_root = jnp.where(side == 0, roots[0], partner)
    right_root = jnp.where(side == 0, partner, roots[0])
    product = jnp.dot(left_root, whole, preferred_element_type=jnp.float32).astype(jnp.bfloat16)
    half = width // 2
    right_half = lax.dynamic_slice_in_dim(right_root, side * half, half, 1)
    portion = jnp.dot(product, right_half, preferred_element_type=jnp.float32).astype(jnp.bfloat16)
    moved = lax.all_to_all(portion[None], "owner", split_axis=1, concat_axis=0, tiled=True)
    update = moved.reshape(blocks, 2, rows, half).transpose(0, 2, 1, 3).reshape(blocks, rows, width)
    fresh = BETA * stats[0] + (1.0 - BETA) * (gram / width)
    solved = inverse_root(fresh)
    chosen = jnp.where(flag == 1, solved.astype(jnp.bfloat16), roots[0])
    return (fresh[None], chosen[None], update)


def solution(mesh):
    placed = (
        P("dp", None, "owner", None),
        P(("dp", "owner"), None, None),
        P(("dp", "owner"), None, None),
        P("dp"),
    )
    return jax.shard_map(
        local,
        mesh=mesh,
        in_specs=placed,
        out_specs=(
            P(("dp", "owner"), None, None),
            P(("dp", "owner"), None, None),
            P("dp", "owner", None),
        ),
        check_vma=False,
    )
```

profile of v0, /device:TPU:1, one launch (start us, length us, event | category | flops | bytes accessed | tf_op | source)
XLA Modules:
  0.0 136.4 jit_solution(5005526059796600987)
XLA Ops:
  0.6 47.6 %all_to_all.23 = bf16[8,1,16,16,512]{4,3,2,1,0:T(8,128)(2,1)S(1)} all-to-all(bf16[8,1,16,16,512]{4,3,2,1,0:T(8,128)(2,1)} %bitcast.57), channel_id=1, replica_groups=mesh['dp'=8,'owner'=32] {'dp'}, dimensions={0} | all-to-all | bytes 4194304 | tf_op jit(solution)/shard_map/all_to_all | solution.py:19
  48.2 0.0 copy-start.3
  48.2 0.0 copy-start
  48.2 0.4 reduce_sum.21
  48.6 0.9 broadcast_in_dim.12
  49.4 23.7 %all-to-all-start.1 = ((bf16[32,16,512]{2,1,0:T(8,128)(2,1)}), bf16[32,16,512]{2,1,0:T(8,128)(2,1)S(1)}, u32[]{:S(2)}, u32[]{:S(2)}) async-start(bf16[32,16,512]{2,1,0:T(8,128)(2,1)} %bitcast.2), calls=%async_computation.1 | async-start | bytes 1048576 | tf_op jit(solution)/shard_map/all_to_all | solution.py:53
  73.1 0.3 collective-permute-start
  73.5 0.0 copy-done.3
  73.5 0.6 dynamic_slice.7
  74.7 15.2 %all-to-all-done.1 = bf16[32,16,512]{2,1,0:T(8,128)(2,1)S(1)} async-done(((bf16[32,16,512]{2,1,0:T(8,128)(2,1)}), bf16[32,16,512]{2,1,0:T(8,128)(2,1)S(1)}, u32[]{:S(2)}, u32[]{:S(2)}) %all-to-all-start.1) | async-done | bytes 524320 | tf_op jit(solution)/shard_map/all_to_all | solution.py:53
  89.9 0.2 copy.16
  90.2 0.0 copy-done
  90.2 1.2 multiply_reduce_fusion
  91.4 0.0 copy-start.1
  92.1 0.0 collective-permute-done
  92.1 1.9 %fusion.6 = bf16[1,512,256]{2,1,0:T(8,128)(2,1)S(1)} fusion(bf16[512,512]{1,0:T(8,128)(2,1)S(1)} %bitcast.55, bf16[1,512,512]{2,1,0:T(8,128)(2,1)} %param.6, bf16[1,512,512]{2,1,0:T(8,128)(2,1)} %collective-permute-done, pred[]{:T(512)S(6)} %eq.26, bf16[512,512]{1,0:T(8,128)(2,1)} %bitcast.61, s32[]{:T(128)S(6)} %select_n.56, bf16[512,512]{1,0:T(8,128)(2,1)} %bitcast.10), kind=kOutput, calls=%fused_computation.14 | convolution fusion | flops 403439616 | bytes 2360832 | tf_op jit(solution)/shard_map/dot_general | solution.py:62
  94.0 0.4 copy.22
  94.5 0.5 broadcast.126
  95.0 2.2 %reduce.2 = bf16[512,256]{1,0:T(8,128)(2,1)S(1)} reduce(bf16[512,1,256]{2,1,0:T(2,128)(2,1)S(1)} %bitcast.58, bf16[]{:T(256)} %broadcast.126), dimensions={1}, to_apply=%bitcast.52.reduce_sub_computation | reduce | bytes 524290
  97.2 0.8 reshape.33
  98.0 3.9 %all-to-all-start.2 = ((bf16[32,2,2048]{2,1,0:T(2,128)(2,1)}), bf16[32,2,2048]{2,1,0:T(2,128)(2,1)S(1)}, u32[]{:S(2)}, u32[]{:S(2)}) async-start(bf16[32,2,2048]{2,1,0:T(2,128)(2,1)} %reshape.33), calls=%async_computation.2 | async-start | bytes 524288 | tf_op jit(solution)/shard_map/all_to_all | solution.py:63
  101.9 2.0 %fusion.25 = f32[512,512]{1,0:T(8,128)S(1)} fusion(f32[512,512]{1,0:T(8,128)S(1)} %get-tuple-element.4, f32[]{:T(128)S(6)} %sqrt.3), kind=kOutput, calls=%fused_computation.29 | convolution fusion | flops 1611923456 | bytes 2097156 | tf_op jit(solution)/shard_map/dot_general | solution.py:39
  103.9 1.9 %fusion.11 = f32[512,512]{1,0:T(8,128)S(1)} fusion(f32[]{:T(128)S(6)} %pow.3, f32[512,512]{1,0:T(8,128)S(1)} %get-tuple-element.4, f32[]{:T(128)S(6)} %sqrt.3), kind=kOutput, calls=%fused_computation.19 | convolution fusion | flops 1612447744 | bytes 2097160 | tf_op jit(solution)/shard_map/dot_general | solution.py:37
  105.8 1.8 %fusion.88 = f32[512,512]{1,0:T(8,128)S(1)} fusion(f32[512,512]{1,0:T(8,128)S(1)} %fusion.25), kind=kOutput, calls=%fused_computation.91 | convolution fusion | flops 1610612736 | bytes 2097152 | tf_op jit(solution)/shard_map/dot_general | solution.py:40
  107.6 0.0 copy-done.1
  107.6 1.9 %fusion.87 = f32[512,512]{1,0:T(8,128)S(1)} fusion(f32[512,512]{1,0:T(8,128)S(1)} %fusion.88, f32[512,512]{1,0:T(8,128)S(1)} %get-tuple-element.4, f32[]{:T(128)S(6)} %sqrt.3), kind=kOutput, calls=%fused_computation.89 | convolution fusion | flops 1610874880 | bytes 3145732 | tf_op jit(solution)/shard_map/dot_general | solution.py:41
  109.5 1.9 %fusion.21 = f32[512,512]{1,0:T(8,128)S(1)} fusion(f32[512,512]{1,0:T(8,128)S(1)} %fusion.87), kind=kOutput, calls=%fused_computation.27 | convolution fusion | flops 1611661312 | bytes 2097152 | tf_op jit(solution)/shard_map/dot_general | solution.py:39
  111.4 1.9 %fusion.23 = f32[512,512]{1,0:T(8,128)S(1)} fusion(f32[512,512]{1,0:T(8,128)S(1)} %fusion.11, f32[512,512]{1,0:T(8,128)S(1)} %fusion.87), kind=kOutput, calls=%fused_computation.28 | convolution fusion | flops 1611661312 | bytes 3145728 | tf_op jit(solution)/shard_map/dot_general | solution.py:37
  113.3 1.8 %fusion.89 = f32[512,512]{1,0:T(8,128)S(1)} fusion(f32[512,512]{1,0:T(8,128)S(1)} %fusion.21), kind=kOutput, calls=%fused_computation.92 | convolution fusion | flops 1610612736 | bytes 2097152 | tf_op jit(solution)/shard_map/dot_general | solution.py:40
  115.2 2.1 %fusion.90 = f32[512,512]{1,0:T(8,128)S(1)} fusion(f32[512,512]{1,0:T(8,128)S(1)} %fusion.89, f32[512,512]{1,0:T(8,128)S(1)} %fusion.87), kind=kOutput, calls=%fused_computation.93 | convolution fusion | flops 1610612736 | bytes 3145728 | tf_op jit(solution)/shard_map/dot_general | solution.py:41
  117.3 1.9 %fusion.17 = f32[512,512]{1,0:T(8,128)S(1)} fusion(f32[512,512]{1,0:T(8,128)S(1)} %fusion.90), kind=kOutput, calls=%fused_computation.25 | convolution fusion | flops 1611661312 | bytes 2097152 | tf_op jit(solution)/shard_map/dot_general | solution.py:39
  119.2 1.9 %fusion.19 = f32[512,512]{1,0:T(8,128)S(1)} fusion(f32[512,512]{1,0:T(8,128)S(1)} %fusion.23, f32[512,512]{1,0:T(8,128)S(1)} %fusion.90), kind=kOutput, calls=%fused_computation.26 | convolution fusion | flops 1611661312 | bytes 3145728 | tf_op jit(solution)/shard_map/dot_general | solution.py:37
  121.1 1.8 %fusion.91 = f32[512,512]{1,0:T(8,128)S(1)} fusion(f32[512,512]{1,0:T(8,128)S(1)} %fusion.17), kind=kOutput, calls=%fused_computation.94 | convolution fusion | flops 1610612736 | bytes 2097152 | tf_op jit(solution)/shard_map/dot_general | solution.py:40
  123.0 1.8 %fusion.92 = f32[512,512]{1,0:T(8,128)S(1)} fusion(f32[512,512]{1,0:T(8,128)S(1)} %fusion.91, f32[512,512]{1,0:T(8,128)S(1)} %fusion.90), kind=kOutput, calls=%fused_computation.95 | convolution fusion | flops 1610612736 | bytes 3145728 | tf_op jit(solution)/shard_map/dot_general | solution.py:41
  124.8 1.9 %fusion.13 = f32[512,512]{1,0:T(8,128)S(1)} fusion(f32[512,512]{1,0:T(8,128)S(1)} %fusion.92), kind=kOutput, calls=%fused_computation.23 | convolution fusion | flops 1611661312 | bytes 2097152 | tf_op jit(solution)/shard_map/dot_general | solution.py:39
  126.7 1.9 %fusion.15 = f32[512,512]{1,0:T(8,128)S(1)} fusion(f32[512,512]{1,0:T(8,128)S(1)} %fusion.19, f32[512,512]{1,0:T(8,128)S(1)} %fusion.92), kind=kOutput, calls=%fused_computation.24 | convolution fusion | flops 1611661312 | bytes 3145728 | tf_op jit(solution)/shard_map/dot_general | solution.py:37
  128.7 2.1 %fusion.93 = f32[512,512]{1,0:T(8,128)S(1)} fusion(f32[512,512]{1,0:T(8,128)S(1)} %fusion.13), kind=kOutput, calls=%fused_computation.96 | convolution fusion | flops 1610612736 | bytes 2097152 | tf_op jit(solution)/shard_map/dot_general | solution.py:40
  130.8 0.0 copy-start.2
  130.8 1.8 %fusion.1 = f32[512,512]{1,0:T(8,128)S(1)} fusion(f32[512,512]{1,0:T(8,128)S(1)} %fusion.93, f32[512,512]{1,0:T(8,128)S(1)} %fusion.92), kind=kOutput, calls=%fused_computation.7 | convolution fusion | flops 1611661312 | bytes 3145728 | tf_op jit(solution)/shard_map/dot_general | solution.py:41
  132.6 0.0 copy-done.2
  132.7 2.7 %fusion.3 = bf16[1,512,512]{2,1,0:T(8,128)(2,1)} fusion(f32[512,512]{1,0:T(8,128)S(1)} %fusion.15, f32[512,512]{1,0:T(8,128)S(1)} %fusion.1, pred[]{:T(512)} %bitcast.6, bf16[1,512,512]{2,1,0:T(8,128)(2,1)S(1)} %copy-done.2), kind=kOutput, calls=%fused_computation.11 | convolution fusion | flops 1611137024 | bytes 3145729 | tf_op jit(solution)/shard_map/dot_general | solution.py:37
  135.3 0.0 all-to-all-done.2
  135.3 0.3 reshape.34
  135.6 0.7 copy.20
  (1 shorter events, 0.0 us)
Async XLA Ops:
  48.2 25.3 %copy-start.3 = (s32[16]{0:T(128)S(1)}, s32[16]{0:T(128)}, u32[]{:S(2)}) copy-start(s32[16]{0:T(128)} %param.7) | copy-start | bytes 196
  48.2 42.0 %copy-start = (f32[1,512,512]{2,1,0:T(8,128)S(1)}, f32[1,512,512]{2,1,0:T(8,128)}, u32[]{:S(2)}) copy-start(f32[1,512,512]{2,1,0:T(8,128)} %param.5) | copy-start | bytes 3145732
  49.4 40.5 %all-to-all-start.1 = ((bf16[32,16,512]{2,1,0:T(8,128)(2,1)}), bf16[32,16,512]{2,1,0:T(8,128)(2,1)S(1)}, u32[]{:S(2)}, u32[]{:S(2)}) async-start(bf16[32,16,512]{2,1,0:T(8,128)(2,1)} %bitcast.2), calls=%async_computation.1 | async-start | bytes 1048576 | tf_op jit(solution)/shard_map/all_to_all | solution.py:53
  73.1 19.0 %collective-permute-start = (bf16[1,512,512]{2,1,0:T(8,128)(2,1)}, bf16[1,512,512]{2,1,0:T(8,128)(2,1)}, u32[]{:S(2)}, u32[]{:S(2)}) collective-permute-start(bf16[1,512,512]{2,1,0:T(8,128)(2,1)} %param.6), channel_id=1, source_target_pairs={{0,1},{1,0},{2,3},{3,2},{4,5},{5,4},{6,7},{7,6},{8,9},{9,8},{10,11... | collective-permute-start | bytes 1572872 | tf_op jit(solution)/shard_map/ppermute | solution.py:26
  91.4 16.2 %copy-start.1 = (f32[512,512]{1,0:T(8,128)}, f32[512,512]{1,0:T(8,128)S(1)}, u32[]{:S(2)}) copy-start(f32[512,512]{1,0:T(8,128)S(1)} %get-tuple-element.4) | copy-start | bytes 3145732
  98.0 37.4 %all-to-all-start.2 = ((bf16[32,2,2048]{2,1,0:T(2,128)(2,1)}), bf16[32,2,2048]{2,1,0:T(2,128)(2,1)S(1)}, u32[]{:S(2)}, u32[]{:S(2)}) async-start(bf16[32,2,2048]{2,1,0:T(2,128)(2,1)} %reshape.33), calls=%async_computation.2 | async-start | bytes 524288 | tf_op jit(solution)/shard_map/all_to_all | solution.py:63
  130.8 1.9 %copy-start.2 = (bf16[1,512,512]{2,1,0:T(8,128)(2,1)S(1)}, bf16[1,512,512]{2,1,0:T(8,128)(2,1)}, u32[]{:S(2)}) copy-start(bf16[1,512,512]{2,1,0:T(8,128)(2,1)} %param.6) | copy-start | bytes 1572868
where the time goes:
time: 137 us; the launch traced here: 136 us
  blocking collectives  47.6 us (35%)
  matrix products  36.4 us (27%)
  starting transfers between devices  27.9 us (20%)
  waiting for transfers between devices  15.3 us (11%)
  local copies, waits for them, and re-layouts  4.38 us (3%)
  other arithmetic  2.57 us (2%)
  between operations  2.26 us (2%)
    all_to_all x1, blocking collectives, summed_on_arrival(): lax.all_to_all(pieces, axis, split_axis=0, concat_axis=0, tiled=True)  47.6 us
    all_to_all x1, starting transfers between devices, local(): lax.all_to_all(doubled, 'owner', split_axis=0, concat_axis=1, tiled=True)[0]  23.7 us
    all_to_all x1, waiting for transfers between devices, local(): lax.all_to_all(doubled, 'owner', split_axis=0, concat_axis=1, tiled=True)[0]  15.2 us
    dot_general x5, matrix products, inverse_root(): result = jnp.dot(result, factor, precision=lax.Precision.HIGHEST)  10.3 us
    dot_general x4, matrix products, inverse_root(): square = jnp.dot(factor, factor, precision=lax.Precision.HIGHEST)  7.72 us
    dot_general x4, matrix products, inverse_root(): current = jnp.dot(fourth, current, precision=lax.Precision.HIGHEST)  7.65 us
    dot_general x4, matrix products, inverse_root(): fourth = jnp.dot(square, square, precision=lax.Precision.HIGHEST)  7.63 us
    all_to_all x1, starting transfers between devices, local(): lax.all_to_all(portion[None], 'owner', split_axis=1, concat_axis=0, tiled...  3.85 us
  transfers between devices with their start and end apart: 3, of which 1 were waited for; matrix products, arithmetic and copies ran while one was open for 26% of the time, Pallas kernels for 0%

commit v1 on v0

v1 whole, which is shorter than its diff:
```python
import functools

import jax
import jax.numpy as jnp
from jax import lax
from jax.experimental import pallas as pl
from jax.experimental.pallas import tpu as pltpu
from jax.sharding import PartitionSpec as P

MESH = pl.DeviceIdType.MESH
BF = jnp.bfloat16
F32 = jnp.float32
BS = 512
ITERS = 5
BETA = 0.8
NY, NZH, NX, NZL, NC = 4, 2, 4, 4, 2
ROWS = 16
TILE = 128
ORDER = (2, 1, 3, 0)


def kernel(
    gp, stats, roots, refresh,
    new_stats, new_roots, update,
    own, side_p, side_m, r1p, r1m, r2ap, r2am, r2bp, r2bm, zrecv, gfull, st, rt, other,
    m32, mb, x32, xb, n32, nb, wb, prod, upd, root_out,
    load_sem, y_send, y_recv, z_send, z_recv, c_send, c_recv, u_send, u_recv, out_sem,
):
    dp = lax.axis_index("dp")
    owner = lax.axis_index("owner")
    y, zh = dp // NZH, dp % NZH
    x, zl, c = owner // (NZL * NC), (owner // NC) % NZL, owner % NC

    def dev(yy, zz, xx, ll, cc):
        return (yy * NZH + zz, (xx * NZL + ll) * NC + cc)

    up, down, far = (y + 1) % NY, (y + 3) % NY, (y + 2) % NY
    dev_up, dev_down = dev(up, zh, x, zl, c), dev(down, zh, x, zl, c)
    partner = dev(y, zh, x, zl, 1 - c)

    loads = [
        pltpu.make_async_copy(gp.at[y], own, load_sem.at[0]),
        pltpu.make_async_copy(gp.at[up, zh], side_p, load_sem.at[1]),
        pltpu.make_async_copy(gp.at[down, 1 - zh], side_m, load_sem.at[2]),
        pltpu.make_async_copy(stats, st, load_sem.at[3]),
        pltpu.make_async_copy(roots, rt, load_sem.at[4]),
    ]
    for copy in loads:
        copy.start()

    barrier = pltpu.get_barrier_semaphore()
    count = 0
    for peer in (dev_up, dev_down, partner):
        pl.semaphore_signal(barrier, inc=1, device_id=peer, device_id_type=MESH)
        count += 1
    for h in range(NZH):
        for k in range(NX):
            for l in range(NZL):
                if (h, k, l) != (0, 0, 0):
                    peer = dev(y, (zh + h) % NZH, (x + k) % NX, (zl + l) % NZL, c)
                    pl.semaphore_signal(barrier, inc=1, device_id=peer, device_id_type=MESH)
                    count += 1
    pl.semaphore_wait(barrier, count)

    def remote(src, dst, send, recv, to):
        copy = pltpu.make_async_remote_copy(
            src_ref=src, dst_ref=dst, send_sem=send, recv_sem=recv, device_id=to, device_id_type=MESH
        )
        copy.start()
        return copy

    y_copies = {}

    def y_send_pair(kind, k):
        xx = (x + ORDER[k]) % NX
        if kind == 0:
            plus, to_p = gp.at[far, zh, xx], r1p.at[k]
            minus, to_m = gp.at[far, 1 - zh, xx], r1m.at[k]
        elif kind == 1:
            plus, to_p = gp.at[up, 1 - zh, xx], r2ap.at[k]
            minus, to_m = gp.at[down, zh, xx], r2am.at[k]
        else:
            plus, to_p = r1p.at[k], r2bp.at[k]
            minus, to_m = r1m.at[k], r2bm.at[k]
        if kind == 2:
            y_copies[0, 0, k].wait_recv()
            r1p[k] = (r1p[k].astype(F32) + side_p[xx].astype(F32)).astype(BF)
        y_copies[kind, 0, k] = remote(plus, to_p, y_send.at[kind, 0, k], y_recv.at[kind, 0, k], dev_up)
        if kind == 2:
            y_copies[0, 1, k].wait_recv()
            r1m[k] = (r1m[k].astype(F32) + side_m[xx].astype(F32)).astype(BF)
        y_copies[kind, 1, k] = remote(minus, to_m, y_send.at[kind, 1, k], y_recv.at[kind, 1, k], dev_down)

    z_copies = {}

    def finish(k):
        xx = (x + ORDER[k]) % NX
        for h in (1, 0):
            zz = (zh + h) % NZH
            direct, chain = (r2am, r2bp) if h == 0 else (r2ap, r2bm)
            y_copies[1, 1 - h, k].wait_recv()
            y_copies[2, h, k].wait_recv()
            total = own[zz, xx].astype(F32) + direct[k].astype(F32) + chain[k].astype(F32)
            own[zz, xx] = total.astype(BF)
            for step in (2, 1, 3, 0):
                l = (zl + step) % NZL
                if (h, ORDER[k], step) == (0, 0, 0):
                    local = pltpu.make_async_copy(own.at[zz, xx, l], zrecv.at[h, k, step], load_sem.at[5])
                    local.start()
                    z_copies[h, k, step] = local
                else:
                    z_copies[h, k, step] = remote(
                        own.at[zz, xx, l], zrecv.at[h, k, step], z_send.at[h, k, step], z_recv.at[h, k, step],
                        dev(y, zz, xx, l, c),
                    )

    y_send_pair(0, 0)
    y_send_pair(0, 1)
    y_send_pair(1, 0)
    loads[1].wait()
    loads[2].wait()
    y_send_pair(2, 0)
    y_send_pair(0, 2)
    y_send_pair(1, 1)
    roots_copy = remote(roots, other, c_send.at[4], c_recv.at[4], partner)
    y_send_pair(2, 1)
    y_send_pair(0, 3)
    y_send_pair(1, 2)
    loads[0].wait()
    finish(0)
    y_send_pair(2, 2)
    y_send_pair(1, 3)
    finish(1)
    y_send_pair(2, 3)
    finish(2)
    finish(3)

    loads[3].wait()
    loads[4].wait()

    c_copies = []
    for k in range(NX):
        xs = (x + NX - ORDER[k]) % NX
        for step in range(NZL):
            ls = (zl + NZL - step) % NZL
            for h in range(NZH):
                if (h, ORDER[k], step) == (0, 0, 0):
                    z_copies[h, k, step].wait()
                else:
                    z_copies[h, k, step].wait_recv()
            total = zrecv[0, k, step].astype(F32) + zrecv[1, k, step].astype(F32)
            gfull[xs, c, ls] = total.astype(BF)
        c_copies.append(remote(gfull.at[xs, c], gfull.at[xs, c], c_send.at[k], c_recv.at[k], partner))
    for copy in c_copies:
        copy.wait_recv()
    roots_copy.wait_recv()

    return_rows = (NX, NC, NZL, ROWS, BS)
    del return_rows
    whole = jnp.concatenate(
        [gfull[a, b, l] for a in range(NX) for l in range(NZL) for b in range(NC)], axis=0
    )
    gw = whole

    def dot(a, b):
        return jnp.dot(a, b, preferred_element_type=F32)

    def do_update(left, right):
        rows = jnp.concatenate([left[pl.ds((2 * j + c) * ROWS, ROWS), :] for j in range(NX * NZL)], axis=0)
        prod[...] = dot(rows, gw).astype(BF)
        upd[...] = dot(prod[...], right[...]).astype(BF).reshape(NX * NZL, ROWS, BS)

    @pl.when(c == 0)
    def _():
        do_update(rt, other)

    @pl.when(c == 1)
    def _():
        do_update(other, rt)

    u_copies = []
    here = x * NZL + zl
    for k in range(NX):
        for step in range(NZL):
            xx, l = (x + ORDER[k]) % NX, (zl + step) % NZL
            j = k * NZL + step
            if (ORDER[k], step) == (0, 0):
                local = pltpu.make_async_copy(upd.at[here], update.at[here], load_sem.at[6])
                local.start()
                u_copies.append(local)
            else:
                u_copies.append(
                    remote(upd.at[xx * NZL + l], update.at[here], u_send.at[j], u_recv.at[j], dev(y, zh, xx, l, c))
                )

    @pl.when(c == 0)
    def _():
        x32[...] = lax.dot_general(gw, gw, (((1,), (1,)), ((), ())), preferred_element_type=F32)

    @pl.when(c == 1)
    def _():
        x32[...] = lax.dot_general(gw, gw, (((0,), (0,)), ((), ())), preferred_element_type=F32)

    fresh = BETA * st[...] + (1.0 - BETA) / BS * x32[...]
    st[...] = fresh
    stats_out = pltpu.make_async_copy(st, new_stats, out_sem.at[0])
    stats_out.start()
    square = jnp.sum(fresh * fresh, axis=0, keepdims=True)
    square = jnp.sum(square, axis=1, keepdims=True) + 1e-6
    inverse = lax.rsqrt(square)
    scale = lax.rsqrt(jnp.sqrt(jnp.sqrt(square)))

    current = st[...] * inverse
    m32[...] = current
    mb[...] = current.astype(BF)
    eye = (
        lax.broadcasted_iota(jnp.int32, (BS, BS), 0) == lax.broadcasted_iota(jnp.int32, (BS, BS), 1)
    ).astype(F32)
    x_now = 1.25 * eye - 0.25 * current
    x32[...] = x_now
    xb[...] = x_now.astype(BF)
    q = 25.0 / 16.0

    def raise_m(first):
        for t in range(0, BS, TILE):
            rows = pl.ds(t, TILE)
            n = (dot(mb[rows, :], mb[...]) - 10.0 * m32[rows, :]) * (1.0 / 16.0)
            n32[rows, :] = n
            nb[rows, :] = n.astype(BF)
        if not first:
            for t in range(0, BS, TILE):
                rows = pl.ds(t, TILE)
                value = 1.25 * x32[rows, :] - 0.25 * dot(xb[rows, :], mb[...])
                x32[rows, :] = value
                xb[rows, :] = value.astype(BF)
        for t in range(0, BS, TILE):
            rows = pl.ds(t, TILE)
            w = 2.0 * q * n32[rows, :] + dot(nb[rows, :], nb[...])
            wb[rows, :] = w.astype(BF)
        for t in range(0, BS, TILE):
            rows = pl.ds(t, TILE)
            m32[rows, :] = q * q * m32[rows, :] + dot(wb[rows, :], mb[...])
        mb[...] = m32[...].astype(BF)

    raise_m(True)

    @pl.loop(0, ITERS - 2)
    def _(_):
        raise_m(False)

    flag = refresh[owner // 2]
    for t in range(0, BS, TILE):
        rows = pl.ds(t, TILE)
        value = 1.25 * x32[rows, :] - 0.25 * dot(xb[rows, :], mb[...])
        value = (value * scale).astype(BF)
        root_out[rows, :] = jnp.where(flag == 1, value, rt[rows, :])
    roots_out = pltpu.make_async_copy(root_out, new_roots, out_sem.at[1])
    roots_out.start()

    for kind in range(3):
        for d in range(2):
            for k in range(NX):
                y_copies[kind, d, k].wait_send()
    for (h, k, step), copy in z_copies.items():
        if (h, ORDER[k], step) != (0, 0, 0):
            copy.wait_send()
    for copy in c_copies:
        copy.wait_send()
    roots_copy.wait_send()
    for copy in u_copies:
        copy.wait()
    stats_out.wait()
    roots_out.wait()


def local(grad_parts, stats, roots, refresh):
    gp = grad_parts.reshape(NY, NZH, NX, NZL, ROWS, BS)
    anywhere = pl.BlockSpec(memory_space=pl.ANY)
    chunk = (NX, NZL, ROWS, BS)
    dma = pltpu.SemaphoreType.DMA
    new_stats, new_roots, update = pl.pallas_call(
        kernel,
        out_shape=(
            jax.ShapeDtypeStruct((BS, BS), F32),
            jax.ShapeDtypeStruct((BS, BS), BF),
            jax.ShapeDtypeStruct((NX * NZL, ROWS, BS), BF),
        ),
        in_specs=[anywhere, anywhere, anywhere, pl.BlockSpec(memory_space=pltpu.SMEM)],
        out_specs=(anywhere, anywhere, anywhere),
        scratch_shapes=[
            pltpu.VMEM((NZH, *chunk), BF),
            *[pltpu.VMEM(chunk, BF) for _ in range(8)],
            pltpu.VMEM((NZH, *chunk), BF),
            pltpu.VMEM((NX, NC, NZL, ROWS, BS), BF),
            pltpu.VMEM((BS, BS), F32),
            pltpu.VMEM((BS, BS), BF),
            pltpu.VMEM((BS, BS), BF),
            pltpu.VMEM((BS, BS), F32),
            pltpu.VMEM((BS, BS), BF),
            pltpu.VMEM((BS, BS), F32),
            pltpu.VMEM((BS, BS), BF),
            pltpu.VMEM((BS, BS), F32),
            pltpu.VMEM((BS, BS), BF),
            pltpu.VMEM((BS, BS), BF),
            pltpu.VMEM((BS // 2, BS), BF),
            pltpu.VMEM((NX * NZL, ROWS, BS), BF),
            pltpu.VMEM((BS, BS), BF),
            dma((7,)),
            dma((3, 2, NX)),
            dma((3, 2, NX)),
            dma((NZH, NX, NZL)),
            dma((NZH, NX, NZL)),
            dma((NX + 1,)),
            dma((NX + 1,)),
            dma((NX * NZL,)),
            dma((NX * NZL,)),
            dma((2,)),
        ],
        compiler_params=pltpu.CompilerParams(
            collective_id=0, has_side_effects=True, vmem_limit_bytes=40 * 1024 * 1024
        ),
        name="shampoo",
    )(gp, stats[0], roots[0], refresh)
    return new_stats[None], new_roots[None], update


def solution(mesh):
    return jax.shard_map(
        local,
        mesh=mesh,
        in_specs=(
            P("dp", None, "owner", None),
            P(("dp", "owner"), None, None),
            P(("dp", "owner"), None, None),
            P("dp"),
        ),
        out_specs=(
            P(("dp", "owner"), None, None),
            P(("dp", "owner"), None, None),
            P("dp", "owner", None),
        ),
        check_vma=False,
    )
```

time: 137 us -> 54.6 us (0.40)
  blocking collectives: 47.6 us -> 0 us
  Pallas kernels: 0 us -> 46.8 us
  matrix products: 36.4 us -> 0 us
  starting transfers between devices: 27.9 us -> 0 us
  waiting for transfers between devices: 15.3 us -> 0 us
  local copies, waits for them, and re-layouts: 4.38 us -> 6.97 us
  other arithmetic: 2.57 us -> 0 us
  between operations: 2.26 us -> 0.65 us
    all_to_all x1 -> x0, blocking collectives: 47.6 us -> none  [summed_on_arrival(): lax.all_to_all(pieces, axis, split_axis=0, concat_axis=0, tiled=True)]
    pallas_call x0 -> x1, Pallas kernels: none -> 46.8 us  [local(): pl.pallas_call(kernel, out_shape=(jax.ShapeDtypeStruct((BS, BS), F32), ja...]
    dot_general x19 -> x0, matrix products: 36.4 us -> none  [the longest x5 10.3 us: inverse_root(): result = jnp.dot(result, factor, precision=lax.Precision.HIGHEST)]
    all_to_all x2 -> x0, starting transfers between devices: 27.6 us -> none  [the longest x1 23.7 us: local(): lax.all_to_all(doubled, 'owner', split_axis=0, concat_axis=1, tiled=True)[0]]
    all_to_all x2 -> x0, waiting for transfers between devices: 15.2 us -> none  [the longest x1 15.2 us: local(): lax.all_to_all(doubled, 'owner', split_axis=0, concat_axis=1, tiled=True)[0]]
    unnamed x12 -> x11, local copies, waits for them, and re-layouts: 1.61 us -> 6.97 us
    unnamed x1 -> x0, other arithmetic: 2.21 us -> none
  transfers between devices with their start and end apart: 3 -> 0, of which waited for: 1 -> 0; matrix products, arithmetic and copies ran while one was open for 26% -> 0% of each run, Pallas kernels for 0% -> 0%
where the time goes in v1:
time: 54.6 us; the launch traced here: 54.4 us
  Pallas kernels  46.8 us (86%)
  local copies, waits for them, and re-layouts  6.97 us (13%)
  between operations  0.65 us (1%)
    pallas_call x1, Pallas kernels, local(): pl.pallas_call(kernel, out_shape=(jax.ShapeDtypeStruct((BS, BS), F32), ja...  46.8 us
    unnamed x11, local copies, waits for them, and re-layouts  6.97 us

profile of v1, /device:TPU:1, one launch (start us, length us, event | category | flops | bytes accessed | tf_op | source)
XLA Modules:
  0.0 54.4 jit_solution(17380016189091083619)
XLA Ops:
  0.6 0.0 copy-start
  0.6 1.6 %copy-done = bf16[1,128,16,512]{3,2,1,0:T(8,128)(2,1)S(1)} copy-done((bf16[1,128,16,512]{3,2,1,0:T(8,128)(2,1)S(1)}, bf16[1,128,16,512]{3,2,1,0:T(8,128)(2,1)}, u32[]{:S(2)}) %copy-start) | copy-done | bytes 2097176
  2.2 0.0 copy-start.1
  2.2 1.2 %copy-done.1 = f32[1,512,512]{2,1,0:T(8,128)S(1)} copy-done((f32[1,512,512]{2,1,0:T(8,128)S(1)}, f32[1,512,512]{2,1,0:T(8,128)}, u32[]{:S(2)}) %copy-start.1) | copy-done | bytes 1048600
  3.4 0.0 copy-start.2
  3.5 1.0 %copy-done.2 = bf16[1,512,512]{2,1,0:T(8,128)(2,1)S(1)} copy-done((bf16[1,512,512]{2,1,0:T(8,128)(2,1)S(1)}, bf16[1,512,512]{2,1,0:T(8,128)(2,1)}, u32[]{:S(2)}) %copy-start.2) | copy-done | bytes 524312
  4.5 0.0 copy-start.3
  4.5 0.7 %copy-done.3 = s32[16]{0:T(128)S(1)} copy-done((s32[16]{0:T(128)S(1)}, s32[16]{0:T(128)}, u32[]{:S(2)}) %copy-start.3) | copy-done | bytes 88
  5.1 46.8 %shampoo.1 = (f32[512,512]{1,0:T(8,128)S(1)}, bf16[512,512]{1,0:T(8,128)(2,1)S(1)}, bf16[16,16,512]{2,1,0:T(8,128)(2,1)S(1)}) custom-call(bf16[4,2,4,4,16,512]{5,4,3,2,1,0:T(8,128)(2,1)S(1)} %bitcast.5, f32[512,512]{1,0:T(8,128)S(1)} %bitcast.7, bf16[512,512]{1,0:T(8,128)(2,1)S(1)} %bitcast.9, s32[16]{0:T(128)S(1)} %copy-done.3), custom_call_target="tpu_custom_call" | custom-call | tf_op jit(solution)/shard_map/shampoo/pallas_call | solution.py:281
  51.9 1.0 %copy.10 = f32[1,512,512]{2,1,0:T(8,128)} copy(f32[1,512,512]{2,1,0:T(8,128)S(1)} %bitcast.6) | data formatting | bytes 2097152
  52.9 0.8 %copy.11 = bf16[1,512,512]{2,1,0:T(8,128)(2,1)} copy(bf16[1,512,512]{2,1,0:T(8,128)(2,1)S(1)} %bitcast.8) | data formatting | bytes 1048576
  53.7 0.7 %copy.12 = bf16[16,16,512]{2,1,0:T(8,128)(2,1)} copy(bf16[16,16,512]{2,1,0:T(8,128)(2,1)S(1)} %get-tuple-element.14) | data formatting | bytes 524288
Async XLA Ops:
  0.6 1.6 %copy-start = (bf16[1,128,16,512]{3,2,1,0:T(8,128)(2,1)S(1)}, bf16[1,128,16,512]{3,2,1,0:T(8,128)(2,1)}, u32[]{:S(2)}) copy-start(bf16[1,128,16,512]{3,2,1,0:T(8,128)(2,1)} %param.4) | copy-start | bytes 6291460
  2.2 1.2 %copy-start.1 = (f32[1,512,512]{2,1,0:T(8,128)S(1)}, f32[1,512,512]{2,1,0:T(8,128)}, u32[]{:S(2)}) copy-start(f32[1,512,512]{2,1,0:T(8,128)} %param.5) | copy-start | bytes 3145732
  3.4 1.0 %copy-start.2 = (bf16[1,512,512]{2,1,0:T(8,128)(2,1)S(1)}, bf16[1,512,512]{2,1,0:T(8,128)(2,1)}, u32[]{:S(2)}) copy-start(bf16[1,512,512]{2,1,0:T(8,128)(2,1)} %param.6) | copy-start | bytes 1572868
  4.5 0.7 %copy-start.3 = (s32[16]{0:T(128)S(1)}, s32[16]{0:T(128)}, u32[]{:S(2)}) copy-start(s32[16]{0:T(128)} %refresh.1) | copy-start | bytes 196

commit v2 on v0

v2 whole, which is shorter than its diff:
```python
import jax
import jax.numpy as jnp
from jax import lax
from jax.experimental import pallas as pl
from jax.experimental.pallas import tpu as pltpu
from jax.sharding import PartitionSpec as P

MESH = pl.DeviceIdType.MESH
BF = jnp.bfloat16
F32 = jnp.float32
BS = 512
ITERS = 5
BETA = 0.8
NY, NZH, NX, NZL, NC = 4, 2, 4, 4, 2
NZ = NZH * NZL
ROWS = 16
TILE = 128
PLUS = (4, 3, 2, 0)
MINUS = (5, 6, 7, 1)
HALVES = 2
WIDE = NX // HALVES
CHUNKS = len(PLUS) * HALVES
AHEAD = 3
LAG = 3
SPREAD = tuple((dx, step) for dx in (2, 1, 3, 0) for step in (2, 3, 1, 0))


def kernel(
    gp, stats, roots, flags,
    new_stats, new_roots, update,
    own, near_p, near_m, r1p, r1m, r2ap, r2am, r2bp, r2bm, zrecv, gfull, st, rt, other,
    m32, mb, x32, xb, n32, nb, wb, prod, upd, refresh,
    load_sem, y_send, y_recv, z_send, z_recv, c_send, c_recv, u_send, u_recv,
):
    dp = lax.axis_index("dp")
    owner = lax.axis_index("owner")
    y, zh = dp // NZH, dp % NZH
    x, zl, c = owner // (NZL * NC), (owner // NC) % NZL, owner % NC
    z = zh * NZL + zl

    def dev(yy, zz, xx, cc):
        return (yy * NZH + zz // NZL, (xx * NZL + zz % NZL) * NC + cc)

    up, down, far = (y + 1) % NY, (y + 3) % NY, (y + 2) % NY
    dev_up, dev_down = dev(up, z, x, c), dev(down, z, x, c)
    partner = dev(y, z, x, 1 - c)

    barrier = pltpu.get_barrier_semaphore()

    def greet(peer):
        pl.semaphore_signal(barrier, inc=1, device_id=peer, device_id_type=MESH)

    for peer in (dev_up, dev_down, partner):
        greet(peer)
    for dx in range(NX):
        for dz in range(NZ):
            if (dx, dz) != (0, 0):
                greet(dev(y, (z + dz) % NZ, (x + dx) % NX, c))

    loads = [
        pltpu.make_async_copy(gp.at[up], near_p, load_sem.at[0]),
        pltpu.make_async_copy(gp.at[down], near_m, load_sem.at[1]),
        pltpu.make_async_copy(gp.at[y], own, load_sem.at[2]),
        pltpu.make_async_copy(roots, rt, load_sem.at[3]),
        pltpu.make_async_copy(stats, st, load_sem.at[4]),
        pltpu.make_async_copy(flags, refresh, load_sem.at[5]),
    ]
    for copy in loads:
        copy.start()

    pl.semaphore_wait(barrier, 2 + NX * NZ)

    def remote(src, dst, send, recv, to):
        copy = pltpu.make_async_remote_copy(
            src_ref=src, dst_ref=dst, send_sem=send, recv_sem=recv, device_id=to, device_id_type=MESH
        )
        copy.start()
        return copy

    def part(ref, dz, k):
        zz = (z + dz) % NZ
        return ref.at[zz // NZL, pl.ds(WIDE * (k % HALVES), WIDE), zz % NZL]

    y_copies = {}

    def y_step(kind, k):
        dzp, dzm = PLUS[k // HALVES], MINUS[k // HALVES]
        if kind == 0:
            plus, to_p = part(gp.at[far], dzp, k), r1p.at[k]
            minus, to_m = part(gp.at[far], dzm, k), r1m.at[k]
        elif kind == 1:
            plus, to_p = part(gp.at[up], dzm, k), r2ap.at[k]
            minus, to_m = part(gp.at[down], dzp, k), r2am.at[k]
        else:
            plus, to_p = r1p.at[k], r2bp.at[k]
            minus, to_m = r1m.at[k], r2bm.at[k]
        if kind == 2:
            y_copies[0, 0, k].wait_recv()
            r1p[k] = (r1p[k].astype(F32) + part(near_p, dzp, k)[...].astype(F32)).astype(BF)
        y_copies[kind, 0, k] = remote(plus, to_p, y_send.at[kind, 0, k], y_recv.at[kind, 0, k], dev_up)
        if kind == 2:
            y_copies[0, 1, k].wait_recv()
            r1m[k] = (r1m[k].astype(F32) + part(near_m, dzm, k)[...].astype(F32)).astype(BF)
        y_copies[kind, 1, k] = remote(minus, to_m, y_send.at[kind, 1, k], y_recv.at[kind, 1, k], dev_down)

    z_copies = []

    def finish(k):
        for side in range(2):
            dz = (PLUS, MINUS)[side][k // HALVES]
            direct, chain = ((r2am, r2bp), (r2ap, r2bm))[side]
            y_copies[1, 1 - side, k].wait_recv()
            y_copies[2, side, k].wait_recv()
            block = part(own, dz, k)
            total = block[...].astype(F32) + direct[k].astype(F32) + chain[k].astype(F32)
            block[...] = total.astype(BF)
            zz = (z + dz) % NZ
            for i in range(WIDE):
                xx = WIDE * (k % HALVES) + i
                src, dst = own.at[zz // NZL, xx, zz % NZL], zrecv.at[dz, x]
                copy = pltpu.make_async_remote_copy(
                    src_ref=src, dst_ref=dst, send_sem=z_send.at[dz, xx], recv_sem=z_recv.at[dz, x],
                    device_id=dev(y, zz, xx, c), device_id_type=MESH,
                )
                if dz == 0:
                    @pl.when(xx != x)
                    def _():
                        copy.start()

                    @pl.when(xx == x)
                    def _():
                        zrecv[0, x] = own[zz // NZL, xx, zz % NZL]
                else:
                    copy.start()
                z_copies.append((dz, xx, copy))

    for k in range(AHEAD):
        y_step(0, k)
    y_step(1, 0)
    roots_copy = remote(roots, other, c_send.at[NZL], c_recv.at[NZL], partner)
    loads[0].wait()
    loads[1].wait()
    for k in range(CHUNKS):
        y_step(2, k)
        if k + AHEAD < CHUNKS:
            y_step(0, k + AHEAD)
        if k + 1 < CHUNKS:
            y_step(1, k + 1)
        if k == LAG:
            loads[2].wait()
        if k >= LAG:
            finish(k - LAG)
    for k in range(CHUNKS - LAG, CHUNKS):
        finish(k)

    c_copies = []
    for first in (2, 3, 0, 1):
        ls = (zl + NZL - first) % NZL
        for dz in (first, first + NZL):
            for dx in range(NX):
                xs = (x + dx) % NX
                arrival = pltpu.make_async_remote_copy(
                    src_ref=zrecv.at[dz, xs], dst_ref=zrecv.at[dz, xs], send_sem=z_send.at[dz, 0],
                    recv_sem=z_recv.at[dz, xs], device_id=partner, device_id_type=MESH,
                )
                if (dz, dx) != (0, 0):
                    arrival.wait_recv()
        gfull[:, ls, c] = (zrecv[first].astype(F32) + zrecv[first + NZL].astype(F32)).astype(BF)
        c_copies.append(
            remote(gfull.at[:, ls, c], gfull.at[:, ls, c], c_send.at[first], c_recv.at[first], partner)
        )
    for copy in loads[3:]:
        copy.wait()
    roots_copy.wait_recv()
    for copy in c_copies:
        copy.wait_recv()

    def dot(a, b):
        return jnp.dot(a, b, preferred_element_type=F32)

    def flat(ref):
        return ref[...].reshape(BS, BS)

    for side, left, right in ((0, rt, other), (1, other, rt)):
        @pl.when(c == side)
        def _():
            prod[...] = dot(left[:, side].reshape(BS // NC, BS), flat(gfull)).astype(BF)
            upd[...] = dot(prod[...], flat(right)).astype(BF).reshape(NX * NZL, ROWS, BS)

    u_copies = []
    here = x * NZL + zl
    swaps = (zl, zl + 1 - 2 * (zl % 2), (zl + 2) % NZL, NZL - 1 - zl)
    for dx, step in SPREAD:
        xx, l = (x + dx) % NX, swaps[step]
        j = dx * NZL + step
        if j == 0:
            update[here] = upd[here]
        else:
            u_copies.append(
                remote(upd.at[xx * NZL + l], update.at[here], u_send.at[j], u_recv.at[j], dev(y, zh * NZL + l, xx, c))
            )

    @pl.when(c == 0)
    def _():
        g = flat(gfull)
        x32[...] = lax.dot_general(g, g, (((1,), (1,)), ((), ())), preferred_element_type=F32)

    @pl.when(c == 1)
    def _():
        g = flat(gfull)
        x32[...] = lax.dot_general(g, g, (((0,), (0,)), ((), ())), preferred_element_type=F32)

    fresh = BETA * st[...] + (1.0 - BETA) / BS * x32[...]
    new_stats[...] = fresh
    square = jnp.sum(fresh * fresh, axis=0, keepdims=True)
    square = jnp.sum(square, axis=1, keepdims=True) + 1e-6
    inverse = lax.rsqrt(square)
    scale = lax.rsqrt(jnp.sqrt(jnp.sqrt(square)))

    current = new_stats[...] * inverse
    m32[...] = current
    mb[...] = current.astype(BF)
    eye = (
        lax.broadcasted_iota(jnp.int32, (BS, BS), 0) == lax.broadcasted_iota(jnp.int32, (BS, BS), 1)
    ).astype(F32)
    x_now = 1.25 * eye - 0.25 * current
    x32[...] = x_now
    xb[...] = x_now.astype(BF)
    q = 25.0 / 16.0

    def raise_m(first):
        for t in range(0, BS, TILE):
            rows = pl.ds(t, TILE)
            n = (dot(mb[rows, :], mb[...]) - 10.0 * m32[rows, :]) * (1.0 / 16.0)
            n32[rows, :] = n
            nb[rows, :] = n.astype(BF)
        if not first:
            for t in range(0, BS, TILE):
                rows = pl.ds(t, TILE)
                value = 1.25 * x32[rows, :] - 0.25 * dot(xb[rows, :], mb[...])
                x32[rows, :] = value
                xb[rows, :] = value.astype(BF)
        for t in range(0, BS, TILE):
            rows = pl.ds(t, TILE)
            w = 2.0 * q * n32[rows, :] + dot(nb[rows, :], nb[...])
            wb[rows, :] = w.astype(BF)
        for t in range(0, BS, TILE):
            rows = pl.ds(t, TILE)
            m32[rows, :] = q * q * m32[rows, :] + dot(wb[rows, :], mb[...])
        mb[...] = m32[...].astype(BF)

    raise_m(True)

    @pl.loop(0, ITERS - 2)
    def _(_):
        raise_m(False)

    flag = refresh[owner // NC]
    old = flat(rt)
    value = 1.25 * x32[...] - 0.25 * dot(xb[...], mb[...])
    new_roots[...] = jnp.where(flag == 1, (value * scale).astype(BF), old)

    for copy in y_copies.values():
        copy.wait_send()
    for dz, xx, copy in z_copies:
        if dz == 0:
            @pl.when(xx != x)
            def _():
                copy.wait_send()
        else:
            copy.wait_send()
    for copy in c_copies:
        copy.wait_send()
    roots_copy.wait_send()
    for copy in u_copies:
        copy.wait()


def write_out(a, b, d, a_out, b_out, d_out, sems):
    copies = [
        pltpu.make_async_copy(src, dst, sems.at[i])
        for i, (src, dst) in enumerate(((a, a_out), (b, b_out), (d, d_out)))
    ]
    for copy in copies:
        copy.start()
    for copy in copies:
        copy.wait()


def local(grad_parts, stats, roots, refresh):
    here = tuple(
        pltpu.with_memory_space_constraint(value, pltpu.HBM)
        for value in (
            grad_parts.reshape(NY, NZH, NX, NZL, ROWS, BS),
            stats[0],
            roots.reshape(NX * NZL, NC, ROWS, BS),
            refresh,
        )
    )
    hbm = pl.BlockSpec(memory_space=pltpu.HBM)
    vmem = pl.BlockSpec(memory_space=pltpu.VMEM)
    everything = (NZH, NX, NZL, ROWS, BS)
    pieces = (CHUNKS, WIDE, ROWS, BS)
    whole = (NX * NZL, NC, ROWS, BS)
    square = (BS, BS)
    dma = pltpu.SemaphoreType.DMA
    outs = ((square, F32), (square, BF), ((NX * NZL, ROWS, BS), BF))
    done = pl.pallas_call(
        kernel,
        out_shape=tuple(pltpu.VMEM(shape, kind) for shape, kind in outs),
        in_specs=[hbm] * 4,
        out_specs=(vmem,) * 3,
        scratch_shapes=[
            *[pltpu.VMEM(everything, BF) for _ in range(3)],
            *[pltpu.VMEM(pieces, BF) for _ in range(6)],
            pltpu.VMEM((NZ, NX, ROWS, BS), BF),
            pltpu.VMEM((NX, NZL, NC, ROWS, BS), BF),
            pltpu.VMEM(square, F32),
            pltpu.VMEM(whole, BF),
            pltpu.VMEM(whole, BF),
            pltpu.VMEM(square, F32),
            pltpu.VMEM(square, BF),
            pltpu.VMEM(square, F32),
            pltpu.VMEM(square, BF),
            pltpu.VMEM(square, F32),
            pltpu.VMEM(square, BF),
            pltpu.VMEM(square, BF),
            pltpu.VMEM((BS // NC, BS), BF),
            pltpu.VMEM((NX * NZL, ROWS, BS), BF),
            pltpu.SMEM((NX * NZL,), jnp.int32),
            dma((6,)),
            dma((3, 2, CHUNKS)),
            dma((3, 2, CHUNKS)),
            dma((NZ, NX)),
            dma((NZ, NX)),
            dma((NZL + 1,)),
            dma((NZL + 1,)),
            dma((NX * NZL,)),
            dma((NX * NZL,)),
        ],
        compiler_params=pltpu.CompilerParams(
            collective_id=0, has_side_effects=True, vmem_limit_bytes=40 * 1024 * 1024
        ),
        name="shampoo",
    )(*here)
    new_stats, new_roots, update = pl.pallas_call(
        write_out,
        out_shape=tuple(pltpu.HBM(shape, kind) for shape, kind in outs),
        in_specs=[vmem] * 3,
        out_specs=(hbm,) * 3,
        scratch_shapes=[dma((3,))],
        name="write_out",
    )(*(pltpu.with_memory_space_constraint(value, pltpu.VMEM) for value in done))
    return new_stats[None], new_roots[None], update


def solution(mesh):
    placed = (
        P("dp", None, "owner", None),
        P(("dp", "owner"), None, None),
        P(("dp", "owner"), None, None),
        P("dp"),
    )
    return jax.shard_map(
        local,
        mesh=mesh,
        in_specs=placed,
        out_specs=(
            P(("dp", "owner"), None, None),
            P(("dp", "owner"), None, None),
            P("dp", "owner", None),
        ),
        check_vma=False,
    )
```

time: 137 us -> 48.1 us (0.35)
  blocking collectives: 47.6 us -> 0 us
  Pallas kernels: 0 us -> 47.3 us
  matrix products: 36.4 us -> 0 us
  starting transfers between devices: 27.9 us -> 0 us
  waiting for transfers between devices: 15.3 us -> 0 us
  local copies, waits for them, and re-layouts: 4.38 us -> 0 us
  other arithmetic: 2.57 us -> 0 us
  between operations: 2.26 us -> 0.64 us
    all_to_all x1 -> x0, blocking collectives: 47.6 us -> none  [summed_on_arrival(): lax.all_to_all(pieces, axis, split_axis=0, concat_axis=0, tiled=True)]
    pallas_call x0 -> x2, Pallas kernels: none -> 47.3 us  [the longest x1 46.1 us: local(): pl.pallas_call(kernel, out_shape=tuple((pltpu.VMEM(shape, kind) for shape...]
    dot_general x19 -> x0, matrix products: 36.4 us -> none  [the longest x5 10.3 us: inverse_root(): result = jnp.dot(result, factor, precision=lax.Precision.HIGHEST)]
    all_to_all x2 -> x0, starting transfers between devices: 27.6 us -> none  [the longest x1 23.7 us: local(): lax.all_to_all(doubled, 'owner', split_axis=0, concat_axis=1, tiled=True)[0]]
    all_to_all x2 -> x0, waiting for transfers between devices: 15.2 us -> none  [the longest x1 15.2 us: local(): lax.all_to_all(doubled, 'owner', split_axis=0, concat_axis=1, tiled=True)[0]]
    unnamed x1 -> x0, other arithmetic: 2.21 us -> none
    unnamed x12 -> x0, local copies, waits for them, and re-layouts: 1.61 us -> none
  transfers between devices with their start and end apart: 3 -> 0, of which waited for: 1 -> 0; matrix products, arithmetic and copies ran while one was open for 26% -> 0% of each run, Pallas kernels for 0% -> 0%
where the time goes in v2:
time: 48.1 us; the launch traced here: 48 us
  Pallas kernels  47.3 us (98%)
  between operations  0.64 us (1%)
    pallas_call x1, Pallas kernels, local(): pl.pallas_call(kernel, out_shape=tuple((pltpu.VMEM(shape, kind) for shape...  46.1 us
    pallas_call x1, Pallas kernels, local(): pl.pallas_call(write_out, out_shape=tuple((pltpu.HBM(shape, kind) for sha...  1.25 us

profile of v2, /device:TPU:1, one launch (start us, length us, event | category | flops | bytes accessed | tf_op | source)
XLA Modules:
  0.0 48.0 jit_solution(2221013997758215656)
XLA Ops:
  0.6 46.1 %shampoo.1 = (f32[512,512]{1,0:T(8,128)S(1)}, bf16[512,512]{1,0:T(8,128)(2,1)S(1)}, bf16[16,16,512]{2,1,0:T(8,128)(2,1)S(1)}) custom-call(bf16[4,2,4,4,16,512]{5,4,3,2,1,0:T(8,128)(2,1)} %bitcast.5, f32[512,512]{1,0:T(8,128)} %bitcast.6, bf16[16,2,16,512]{3,2,1,0:T(8,128)(2,1)} %bitcast.7, s32[16]{0:T(128)} %flags.1), custom_call_target="tpu_custom_call" | custom-call | tf_op jit(solution)/shard_map/shampoo/pallas_call | solution.py:308
  46.7 1.2 %write_out.1 = (f32[512,512]{1,0:T(8,128)}, bf16[512,512]{1,0:T(8,128)(2,1)}, bf16[16,16,512]{2,1,0:T(8,128)(2,1)}) custom-call(f32[512,512]{1,0:T(8,128)S(1)} %get-tuple-element.9.a, bf16[512,512]{1,0:T(8,128)(2,1)S(1)} %get-tuple-element.10.b, bf16[16,16,512]{2,1,0:T(8,128)(2,1)S(1)} %get-tuple-element.11.d), custom_call_target="tpu_custom_call" | custom-call | tf_op jit(solution)/shard_map/write_out/pallas_call | solution.py:346

commit v3 on v2

--- a/solution.py
+++ b/solution.py
@@ -15,12 +15,13 @@
 NZ = NZH * NZL
 ROWS = 16
 TILE = 128
-PLUS = (4, 3, 2, 0)
-MINUS = (5, 6, 7, 1)
+PLUS = (((1, 0), (0, 3), (0, 0), (1, 1)), ((1, 0), (1, 1), (0, 2), (0, 0)))
+MINUS = (((1, 2), (0, 2), (0, 1), (1, 3)), ((1, 2), (1, 3), (0, 3), (0, 1)))
 HALVES = 2
 WIDE = NX // HALVES
-CHUNKS = len(PLUS) * HALVES
+CHUNKS = len(PLUS[0]) * HALVES
 AHEAD = 3
+ROUNDS = ((0,), (1,), (2,), (3, 4), (), (), (), ())
 LAG = 3
 SPREAD = tuple((dx, step) for dx in (2, 1, 3, 0) for step in (2, 3, 1, 0))
 
@@ -30,7 +31,7 @@
     new_stats, new_roots, update,
     own, near_p, near_m, r1p, r1m, r2ap, r2am, r2bp, r2bm, zrecv, gfull, st, rt, other,
     m32, mb, x32, xb, n32, nb, wb, prod, upd, refresh,
-    load_sem, y_send, y_recv, z_send, z_recv, c_send, c_recv, u_send, u_recv,
+    load_sem, y_send, y_recv, z_send, z_recv, c_send, c_recv, u_send, u_recv, ring,
 ):
     dp = lax.axis_index("dp")
     owner = lax.axis_index("owner")
@@ -50,12 +51,10 @@
     def greet(peer):
         pl.semaphore_signal(barrier, inc=1, device_id=peer, device_id_type=MESH)
 
-    for peer in (dev_up, dev_down, partner):
+    z_pair = (dev(y, (z + 1) % NZ, x, c), dev(y, (z + NZ - 1) % NZ, x, c))
+    x_pair = (dev(y, z, (x + 1) % NX, c), dev(y, z, (x + NX - 1) % NX, c))
+    for peer in (dev_up, dev_down, partner, *z_pair, *x_pair):
         greet(peer)
-    for dx in range(NX):
-        for dz in range(NZ):
-            if (dx, dz) != (0, 0):
-                greet(dev(y, (z + dz) % NZ, (x + dx) % NX, c))
 
     loads = [
         pltpu.make_async_copy(gp.at[up], near_p, load_sem.at[0]),
@@ -68,7 +67,16 @@
     for copy in loads:
         copy.start()
 
-    pl.semaphore_wait(barrier, 2 + NX * NZ)
+    pl.semaphore_wait(barrier, 7)
+
+    rounds = (z_pair, z_pair, z_pair, x_pair, x_pair)
+
+    def tell(i):
+        for peer in rounds[i]:
+            pl.semaphore_signal(ring.at[i], inc=1, device_id=peer, device_id_type=MESH)
+
+    def hear(i):
+        pl.semaphore_wait(ring.at[i], 2)
 
     def remote(src, dst, send, recv, to):
         copy = pltpu.make_async_remote_copy(
@@ -77,14 +85,21 @@
         copy.start()
         return copy
 
-    def part(ref, dz, k):
-        zz = (z + dz) % NZ
-        return ref.at[zz // NZL, pl.ds(WIDE * (k % HALVES), WIDE), zz % NZL]
+    def offset(table, k):
+        (h0, s0), (h1, s1) = table[0][k // HALVES], table[1][k // HALVES]
+        return h0 + zh * (h1 - h0), s0 + zh * (s1 - s0)
+
+    def place(off):
+        return (zh + off[0]) % NZH, (zl + off[1]) % NZL
+
+    def part(ref, off, k):
+        zzh, zzl = place(off)
+        return ref.at[zzh, pl.ds(WIDE * (k % HALVES), WIDE), zzl]
 
     y_copies = {}
 
     def y_step(kind, k):
-        dzp, dzm = PLUS[k // HALVES], MINUS[k // HALVES]
+        dzp, dzm = offset(PLUS, k), offset(MINUS, k)
         if kind == 0:
             plus, to_p = part(gp.at[far], dzp, k), r1p.at[k]
             minus, to_m = part(gp.at[far], dzm, k), r1m.at[k]
@@ -107,37 +122,42 @@
 
     def finish(k):
         for side in range(2):
-            dz = (PLUS, MINUS)[side][k // HALVES]
+            table = (PLUS, MINUS)[side]
+            off = offset(table, k)
             direct, chain = ((r2am, r2bp), (r2ap, r2bm))[side]
             y_copies[1, 1 - side, k].wait_recv()
             y_copies[2, side, k].wait_recv()
-            block = part(own, dz, k)
+            block = part(own, off, k)
             total = block[...].astype(F32) + direct[k].astype(F32) + chain[k].astype(F32)
             block[...] = total.astype(BF)
-            zz = (z + dz) % NZ
+            zzh, zzl = place(off)
             for i in range(WIDE):
                 xx = WIDE * (k % HALVES) + i
-                src, dst = own.at[zz // NZL, xx, zz % NZL], zrecv.at[dz, x]
                 copy = pltpu.make_async_remote_copy(
-                    src_ref=src, dst_ref=dst, send_sem=z_send.at[dz, xx], recv_sem=z_recv.at[dz, x],
-                    device_id=dev(y, zz, xx, c), device_id_type=MESH,
+                    src_ref=own.at[zzh, xx, zzl], dst_ref=zrecv.at[off[0], off[1], x],
+                    send_sem=z_send.at[side, k, i], recv_sem=z_recv.at[off[0], off[1], x],
+                    device_id=dev(y, zzh * NZL + zzl, xx, c), device_id_type=MESH,
                 )
-                if dz == 0:
-                    @pl.when(xx != x)
+                if (0, 0) in (table[0][k // HALVES], table[1][k // HALVES]):
+                    stays = jnp.logical_and(jnp.logical_and(off[0] == 0, off[1] == 0), xx == x)
+
+                    @pl.when(jnp.logical_not(stays))
                     def _():
                         copy.start()
 
-                    @pl.when(xx == x)
+                    @pl.when(stays)
                     def _():
-                        zrecv[0, x] = own[zz // NZL, xx, zz % NZL]
+                        zrecv[0, 0, x] = own[zzh, xx, zzl]
                 else:
+                    stays = None
                     copy.start()
-                z_copies.append((dz, xx, copy))
+                z_copies.append((stays, copy))
 
     for k in range(AHEAD):
         y_step(0, k)
     y_step(1, 0)
     roots_copy = remote(roots, other, c_send.at[NZL], c_recv.at[NZL], partner)
+    tell(0)
     loads[0].wait()
     loads[1].wait()
     for k in range(CHUNKS):
@@ -146,6 +166,10 @@
             y_step(0, k + AHEAD)
         if k + 1 < CHUNKS:
             y_step(1, k + 1)
+        for i in ROUNDS[k]:
+            hear(i)
+            if i + 1 < len(rounds):
+                tell(i + 1)
         if k == LAG:
             loads[2].wait()
         if k >= LAG:
@@ -154,20 +178,20 @@
         finish(k)
 
     c_copies = []
-    for first in (2, 3, 0, 1):
-        ls = (zl + NZL - first) % NZL
-        for dz in (first, first + NZL):
+    for step in (2, 3, 0, 1):
+        ls = (zl + NZL - step) % NZL
+        for h in range(NZH):
             for dx in range(NX):
                 xs = (x + dx) % NX
                 arrival = pltpu.make_async_remote_copy(
-                    src_ref=zrecv.at[dz, xs], dst_ref=zrecv.at[dz, xs], send_sem=z_send.at[dz, 0],
-                    recv_sem=z_recv.at[dz, xs], device_id=partner, device_id_type=MESH,
+                    src_ref=zrecv.at[h, step, xs], dst_ref=zrecv.at[h, step, xs], send_sem=z_send.at[0, 0, 0],
+                    recv_sem=z_recv.at[h, step, xs], device_id=partner, device_id_type=MESH,
                 )
-                if (dz, dx) != (0, 0):
+                if (h, step, dx) != (0, 0, 0):
                     arrival.wait_recv()
-        gfull[:, ls, c] = (zrecv[first].astype(F32) + zrecv[first + NZL].astype(F32)).astype(BF)
+        gfull[:, ls, c] = (zrecv[0, step].astype(F32) + zrecv[1, step].astype(F32)).astype(BF)
         c_copies.append(
-            remote(gfull.at[:, ls, c], gfull.at[:, ls, c], c_send.at[first], c_recv.at[first], partner)
+            remote(gfull.at[:, ls, c], gfull.at[:, ls, c], c_send.at[step], c_recv.at[step], partner)
         )
     for copy in loads[3:]:
         copy.wait()
@@ -262,13 +286,13 @@
 
     for copy in y_copies.values():
         copy.wait_send()
-    for dz, xx, copy in z_copies:
-        if dz == 0:
-            @pl.when(xx != x)
+    for stays, copy in z_copies:
+        if stays is None:
+            copy.wait_send()
+        else:
+            @pl.when(jnp.logical_not(stays))
             def _():
                 copy.wait_send()
-        else:
-            copy.wait_send()
     for copy in c_copies:
         copy.wait_send()
     roots_copy.wait_send()
@@ -313,7 +337,7 @@
         scratch_shapes=[
             *[pltpu.VMEM(everything, BF) for _ in range(3)],
             *[pltpu.VMEM(pieces, BF) for _ in range(6)],
-            pltpu.VMEM((NZ, NX, ROWS, BS), BF),
+            pltpu.VMEM((NZH, NZL, NX, ROWS, BS), BF),
             pltpu.VMEM((NX, NZL, NC, ROWS, BS), BF),
             pltpu.VMEM(square, F32),
             pltpu.VMEM(whole, BF),
@@ -331,12 +355,13 @@
             dma((6,)),
             dma((3, 2, CHUNKS)),
             dma((3, 2, CHUNKS)),
-            dma((NZ, NX)),
-            dma((NZ, NX)),
+            dma((2, CHUNKS, WIDE)),
+            dma((NZH, NZL, NX)),
             dma((NZL + 1,)),
             dma((NZL + 1,)),
             dma((NX * NZL,)),
             dma((NX * NZL,)),
+            pltpu.SemaphoreType.REGULAR((5,)),
         ],
         compiler_params=pltpu.CompilerParams(
             collective_id=0, has_side_effects=True, vmem_limit_bytes=40 * 1024 * 1024

time: 48.1 us -> 45.2 us (0.940)
  Pallas kernels: 47.3 us -> 44.4 us
    pallas_call x1, Pallas kernels: 46.1 us -> 43.2 us  [local(): pl.pallas_call(kernel, out_shape=tuple((pltpu.VMEM(shape, kind) for shape...]
where the time goes in v3:
time: 45.2 us; the launch traced here: 45.1 us
  Pallas kernels  44.4 us (98%)
  between operations  0.64 us (1%)
    pallas_call x1, Pallas kernels, local(): pl.pallas_call(kernel, out_shape=tuple((pltpu.VMEM(shape, kind) for shape...  43.2 us
    pallas_call x1, Pallas kernels, local(): pl.pallas_call(write_out, out_shape=tuple((pltpu.HBM(shape, kind) for sha...  1.25 us

profile of v3, /device:TPU:1, one launch (start us, length us, event | category | flops | bytes accessed | tf_op | source)
XLA Modules:
  0.0 45.1 jit_solution(6163293346435624123)
XLA Ops:
  0.6 43.2 %shampoo.1 = (f32[512,512]{1,0:T(8,128)S(1)}, bf16[512,512]{1,0:T(8,128)(2,1)S(1)}, bf16[16,16,512]{2,1,0:T(8,128)(2,1)S(1)}) custom-call(bf16[4,2,4,4,16,512]{5,4,3,2,1,0:T(8,128)(2,1)} %bitcast.5, f32[512,512]{1,0:T(8,128)} %bitcast.6, bf16[16,2,16,512]{3,2,1,0:T(8,128)(2,1)} %bitcast.7, s32[16]{0:T(128)} %flags.1), custom_call_target="tpu_custom_call" | custom-call | tf_op jit(solution)/shard_map/shampoo/pallas_call | solution.py:332
  43.8 1.2 %write_out.1 = (f32[512,512]{1,0:T(8,128)}, bf16[512,512]{1,0:T(8,128)(2,1)}, bf16[16,16,512]{2,1,0:T(8,128)(2,1)}) custom-call(f32[512,512]{1,0:T(8,128)S(1)} %get-tuple-element.9.a, bf16[512,512]{1,0:T(8,128)(2,1)S(1)} %get-tuple-element.10.b, bf16[16,16,512]{2,1,0:T(8,128)(2,1)S(1)} %get-tuple-element.11.d), custom_call_target="tpu_custom_call" | custom-call | tf_op jit(solution)/shard_map/write_out/pallas_call | solution.py:371

commit v4 on v3

--- a/solution.py
+++ b/solution.py
@@ -20,9 +20,12 @@
 HALVES = 2
 WIDE = NX // HALVES
 CHUNKS = len(PLUS[0]) * HALVES
-AHEAD = 3
-ROUNDS = ((0,), (1,), (2,), (3, 4), (), (), (), ())
-LAG = 3
+AHEAD = 4
+SWAP = 4
+LOADS = 2
+EARLY = (0,)
+ROUNDS = ((1,), (2,), (3, 4), (), (), (), (), ())
+LAG = 2
 SPREAD = tuple((dx, step) for dx in (2, 1, 3, 0) for step in (2, 3, 1, 0))
 
 
@@ -51,10 +54,25 @@
     def greet(peer):
         pl.semaphore_signal(barrier, inc=1, device_id=peer, device_id_type=MESH)
 
-    z_pair = (dev(y, (z + 1) % NZ, x, c), dev(y, (z + NZ - 1) % NZ, x, c))
-    x_pair = (dev(y, z, (x + 1) % NX, c), dev(y, z, (x + NX - 1) % NX, c))
-    for peer in (dev_up, dev_down, partner, *z_pair, *x_pair):
+    def along_z(d):
+        return (z + d < NZ, dev(y, (z + d) % NZ, x, c)), (z >= d, dev(y, (z + NZ - d) % NZ, x, c))
+
+    def along_x(d):
+        return (x + d < NX, dev(y, z, (x + d) % NX, c)), (x >= d, dev(y, z, (x + NX - d) % NX, c))
+
+    def present(pairs):
+        return sum(lax.convert_element_type(there, jnp.int32) for there, _ in pairs)
+
+    def signal_all(pairs, sem):
+        for there, peer in pairs:
+            @pl.when(there)
+            def _():
+                pl.semaphore_signal(sem, inc=1, device_id=peer, device_id_type=MESH)
+
+    for peer in (dev_up, dev_down, partner):
         greet(peer)
+    close = (*along_z(1), *along_x(1))
+    signal_all(close, barrier)
 
     loads = [
         pltpu.make_async_copy(gp.at[up], near_p, load_sem.at[0]),
@@ -64,19 +82,18 @@
         pltpu.make_async_copy(stats, st, load_sem.at[4]),
         pltpu.make_async_copy(flags, refresh, load_sem.at[5]),
     ]
-    for copy in loads:
+    for copy in loads[:LOADS]:
         copy.start()
 
-    pl.semaphore_wait(barrier, 7)
-
-    rounds = (z_pair, z_pair, z_pair, x_pair, x_pair)
+    pl.semaphore_wait(barrier, 3 + present(close))
+
+    rounds = (along_z(1), along_z(2), along_z(4), along_x(1), along_x(2))
 
     def tell(i):
-        for peer in rounds[i]:
-            pl.semaphore_signal(ring.at[i], inc=1, device_id=peer, device_id_type=MESH)
+        signal_all(rounds[i], ring.at[i])
 
     def hear(i):
-        pl.semaphore_wait(ring.at[i], 2)
+        pl.semaphore_wait(ring.at[i], present(rounds[i]))
 
     def remote(src, dst, send, recv, to):
         copy = pltpu.make_async_remote_copy(
@@ -156,11 +173,16 @@
     for k in range(AHEAD):
         y_step(0, k)
     y_step(1, 0)
-    roots_copy = remote(roots, other, c_send.at[NZL], c_recv.at[NZL], partner)
     tell(0)
     loads[0].wait()
     loads[1].wait()
+    for i in EARLY:
+        hear(i)
+        tell(i + 1)
     for k in range(CHUNKS):
+        if k == 0:
+            for copy in loads[LOADS:]:
+                copy.start()
         y_step(2, k)
         if k + AHEAD < CHUNKS:
             y_step(0, k + AHEAD)
@@ -172,6 +194,8 @@
                 tell(i + 1)
         if k == LAG:
             loads[2].wait()
+        if k == SWAP:
+            roots_copy = remote(roots, other, c_send.at[NZL], c_recv.at[NZL], partner)
         if k >= LAG:
             finish(k - LAG)
     for k in range(CHUNKS - LAG, CHUNKS):

time: 45.2 us -> 44.7 us (0.989)
    pallas_call x1, Pallas kernels: 43.2 us -> 42.7 us  [local(): pl.pallas_call(kernel, out_shape=tuple((pltpu.VMEM(shape, kind) for shape...]
where the time goes in v4:
time: 44.7 us; the launch traced here: 44.6 us
  Pallas kernels  44 us (98%)
  between operations  0.64 us (1%)
    pallas_call x1, Pallas kernels, local(): pl.pallas_call(kernel, out_shape=tuple((pltpu.VMEM(shape, kind) for shape...  42.7 us
    pallas_call x1, Pallas kernels, local(): pl.pallas_call(write_out, out_shape=tuple((pltpu.HBM(shape, kind) for sha...  1.25 us

profile of v4, /device:TPU:1, one launch (start us, length us, event | category | flops | bytes accessed | tf_op | source)
XLA Modules:
  0.0 44.6 jit_solution(490379049362562538)
XLA Ops:
  0.6 42.7 %shampoo.1 = (f32[512,512]{1,0:T(8,128)S(1)}, bf16[512,512]{1,0:T(8,128)(2,1)S(1)}, bf16[16,16,512]{2,1,0:T(8,128)(2,1)S(1)}) custom-call(bf16[4,2,4,4,16,512]{5,4,3,2,1,0:T(8,128)(2,1)} %bitcast.5, f32[512,512]{1,0:T(8,128)} %bitcast.6, bf16[16,2,16,512]{3,2,1,0:T(8,128)(2,1)} %bitcast.7, s32[16]{0:T(128)} %flags.1), custom_call_target="tpu_custom_call" | custom-call | tf_op jit(solution)/shard_map/shampoo/pallas_call | solution.py:356
  43.4 1.2 %write_out.1 = (f32[512,512]{1,0:T(8,128)}, bf16[512,512]{1,0:T(8,128)(2,1)}, bf16[16,16,512]{2,1,0:T(8,128)(2,1)}) custom-call(f32[512,512]{1,0:T(8,128)S(1)} %get-tuple-element.9.a, bf16[512,512]{1,0:T(8,128)(2,1)S(1)} %get-tuple-element.10.b, bf16[16,16,512]{2,1,0:T(8,128)(2,1)S(1)} %get-tuple-element.11.d), custom_call_target="tpu_custom_call" | custom-call | tf_op jit(solution)/shard_map/write_out/pallas_call | solution.py:395
